TPU v7x, 256 devices: a whole 4x4x8 slice. The times are simulated.
256 devices in a mesh: scene: 64 (over z_hi, y, x, core), view: 4 (over z_lo).
Axes of the slice: x: 4, y: 4, z: 8 (z_hi: 2, z_lo: 4; z = z_hi * 4 + z_lo), core: 2. Of those that a mesh axis runs over, the one named last changes fastest.
Arguments:
- queries: bfloat16 [64, 4, 512, 1024], P('scene', 'view'), may hold values from -6 to 6
- keys: bfloat16 [64, 4, 512, 1024], P('scene', 'view'), may hold values from -6 to 6
- values: bfloat16 [64, 4, 512, 1024], P('scene', 'view'), may hold values from -6 to 6
- out_grad: bfloat16 [64, 4, 512, 2048], P('scene', 'view'), may hold values from -1.5 to 1.5
- w_out: bfloat16 [1024, 2048], replicated, may hold values from -0.1875 to 0.1875
- bucket_of: int32 [64, 4, 4], P('scene'), may hold values from 0 to 3, as said below
- pair_mask: int32 [64, 4, 4], P('scene'), may hold values from 0 to 1, as said below
Outputs:
- layer_out: bfloat16 [64, 4, 512, 2048], P('scene', 'view')
- grad_queries: bfloat16 [64, 4, 512, 1024], P('scene', 'view')
- grad_keys: bfloat16 [64, 4, 512, 1024], P('scene', 'view')
- grad_values: bfloat16 [64, 4, 512, 1024], P('scene', 'view')
- grad_w_out: bfloat16 [1024, 2048], replicated
Inputs may be any that keep to these rules, and one draw needn't show every extreme that they name: `bucket_of`: each view's 4 blocks lie in 4 different buckets; in every scene one bucket holds a block of every view. pair_mask[s, a, a] = 1 for every view a.
All inputs are finite; a program needn't handle non-finite values.
Results may differ from a plain program's by a relative error of at most 0.008.
Values may be sent and summed in bfloat16 or wider, within the bound.
A program may use at most 128 MiB of HBM per device.

v0:
```python
import math

import jax
import jax.numpy as jnp
from jax import lax
from jax.sharding import PartitionSpec as P

HDIM = 128
BLK = 128


NEG_FILL = -1e30


def head_pass(inputs, allowed, inv_root):
    queries_h, keys_h, values_h, grads_h = inputs
    scores = (
        jnp.einsum("sid,sjd->sij", queries_h, keys_h, preferred_element_type=jnp.float32) * inv_root
    )
    scores = jnp.where(allowed, scores, NEG_FILL)
    peak = jnp.max(scores, axis=-1, keepdims=True)
    exponent = jnp.exp(scores - peak)
    weights = exponent / jnp.sum(exponent, axis=-1, keepdims=True)
    weights_b = weights.astype(jnp.bfloat16)
    attended = jnp.einsum(
        "sij,sjd->sid", weights_b, values_h, preferred_element_type=jnp.float32
    ).astype(jnp.bfloat16)
    grad_weights = jnp.einsum("sid,sjd->sij", grads_h, values_h, preferred_element_type=jnp.float32)
    row_dot = jnp.sum(weights * grad_weights, axis=-1, keepdims=True)
    grad_scores = (weights * (grad_weights - row_dot) * inv_root).astype(jnp.bfloat16)
    grad_query = jnp.einsum(
        "sij,sjd->sid", grad_scores, keys_h, preferred_element_type=jnp.float32
    ).astype(jnp.bfloat16)
    grad_key = jnp.einsum(
        "sij,sid->sjd", grad_scores, queries_h, preferred_element_type=jnp.float32
    ).astype(jnp.bfloat16)
    grad_value = jnp.einsum(
        "sij,sid->sjd", weights_b, grads_h, preferred_element_type=jnp.float32
    ).astype(jnp.bfloat16)
    return (attended, grad_query, grad_key, grad_value)


def body(queries, keys, values, out_grad, w_out, bucket_of, pair_mask):
    view_count = lax.axis_size("view")
    owner_id = lax.axis_index("view")
    scenes_here = queries.shape[0]
    tokens = queries.shape[2]
    width = queries.shape[3]
    heads = width // HDIM
    block_count = tokens // BLK
    rows_all = view_count * BLK
    dest_ids = jnp.arange(view_count, dtype=jnp.int32)
    my_buckets = lax.dynamic_index_in_dim(bucket_of, owner_id, 1, keepdims=False)
    selector = (my_buckets[:, None, :] == dest_ids[None, :, None]).astype(jnp.bfloat16)

    def pack(tensor):
        blocks = tensor.reshape(scenes_here, block_count, BLK, tensor.shape[-1])
        return jnp.einsum(
            "sdb,sbrf->sdrf", selector, blocks, preferred_element_type=jnp.float32
        ).astype(jnp.bfloat16)

    def unpack(tensor):
        blocks = jnp.einsum(
            "sdb,sdrf->sbrf", selector, tensor, preferred_element_type=jnp.float32
        ).astype(jnp.bfloat16)
        return blocks.reshape(scenes_here, 1, tokens, tensor.shape[-1])

    grad_attn = jnp.einsum(
        "svtd,fd->svtf", out_grad, w_out, preferred_element_type=jnp.float32
    ).astype(jnp.bfloat16)
    got_query, got_key, got_value, got_grad = (
        lax.all_to_all(pack(queries), "view", split_axis=1, concat_axis=1, tiled=True),
        lax.all_to_all(pack(keys), "view", split_axis=1, concat_axis=1, tiled=True),
        lax.all_to_all(pack(values), "view", split_axis=1, concat_axis=1, tiled=True),
        lax.all_to_all(pack(grad_attn), "view", split_axis=1, concat_axis=1, tiled=True),
    )
    live_src = jnp.any(bucket_of == owner_id, axis=2)
    allowed_blocks = (pair_mask > 0) & live_src[:, None, :]
    allowed = jnp.repeat(jnp.repeat(allowed_blocks, BLK, axis=1), BLK, axis=2)
    inv_root = 1.0 / math.sqrt(HDIM)

    def split_heads(tensor):
        return tensor.reshape(scenes_here, rows_all, heads, HDIM).transpose(2, 0, 1, 3)

    def join_heads(tensor):
        return tensor.transpose(1, 2, 0, 3).reshape(scenes_here, view_count, BLK, width)

    results = lax.map(
        lambda inputs: head_pass(inputs, allowed, inv_root),
        (
            split_heads(got_query),
            split_heads(got_key),
            split_heads(got_value),
            split_heads(got_grad),
        ),
    )
    back_attended, back_query, back_key, back_value = (
        lax.all_to_all(join_heads(results[0]), "view", split_axis=1, concat_axis=1, tiled=True),
        lax.all_to_all(join_heads(results[1]), "view", split_axis=1, concat_axis=1, tiled=True),
        lax.all_to_all(join_heads(results[2]), "view", split_axis=1, concat_axis=1, tiled=True),
        lax.all_to_all(join_heads(results[3]), "view", split_axis=1, concat_axis=1, tiled=True),
    )
    attended = unpack(back_attended)
    grad_queries = unpack(back_query)
    grad_keys = unpack(back_key)
    grad_values = unpack(back_value)
    layer_out = jnp.einsum(
        "svtf,fd->svtd", attended, w_out, preferred_element_type=jnp.float32
    ).astype(jnp.bfloat16)
    partial_grad = jnp.einsum(
        "svtf,svtd->fd", attended, out_grad, preferred_element_type=jnp.float32
    )
    grad_w_out = lax.psum(partial_grad, ("scene", "view")).astype(jnp.bfloat16)
    return (layer_out, grad_queries, grad_keys, grad_values, grad_w_out)


def solution(mesh):
    placed = (
        P("scene", "view", None, None),
        P("scene", "view", None, None),
        P("scene", "view", None, None),
        P("scene", "view", None, None),
        P(),
        P("scene", None, None),
        P("scene", None, None),
    )
    return jax.shard_map(
        body,
        mesh=mesh,
        in_specs=placed,
        out_specs=(
            P("scene", "view", None, None),
            P("scene", "view", None, None),
            P("scene", "view", None, None),
            P("scene", "view", None, None),
            P(),
        ),
        check_vma=False,
    )
```

profile of v0, /device:TPU:1, one launch (start us, length us, event | category | flops | bytes accessed | tf_op | source)
XLA Modules:
  0.0 468.7 jit_solution(9484183739912808766)
XLA Ops:
  2.2 4.5 fusion.45
  9.4 6.4 %all-to-all-start.3 = ((bf16[1,4,128,1024]{3,2,0,1:T(8,128)(2,1)}), bf16[1,4,128,1024]{3,2,0,1:T(8,128)(2,1)S(1)}, u32[]{:S(2)}, u32[]{:S(2)}) async-start(bf16[1,4,128,1024]{3,2,0,1:T(8,128)(2,1)} %copy.61), calls=%async_computation.3 | async-start | bytes 2097152 | tf_op jit(solution)/shard_map/all_to_all | solution.py:75
  15.9 2.4 fusion.48
  19.5 21.6 %all-to-all-done.3 = bf16[1,4,128,1024]{3,2,0,1:T(8,128)(2,1)S(1)} async-done(((bf16[1,4,128,1024]{3,2,0,1:T(8,128)(2,1)}), bf16[1,4,128,1024]{3,2,0,1:T(8,128)(2,1)S(1)}, u32[]{:S(2)}, u32[]{:S(2)}) %all-to-all-start.3) | async-done | bytes 1048608 | tf_op jit(solution)/shard_map/all_to_all | solution.py:75
  41.1 4.3 all-to-all-start
  45.4 2.4 fusion.49
  49.0 21.6 %all-to-all-done = bf16[1,4,128,1024]{3,2,0,1:T(8,128)(2,1)} async-done(((bf16[1,4,128,1024]{3,2,0,1:T(8,128)(2,1)}), bf16[1,4,128,1024]{3,2,0,1:T(8,128)(2,1)}, u32[]{:S(2)}, u32[]{:S(2)}) %all-to-all-start) | async-done | bytes 1048608 | tf_op jit(solution)/shard_map/all_to_all | solution.py:72
  70.6 4.2 all-to-all-start.1
  74.9 2.4 fusion.50
  78.6 21.6 %all-to-all-done.1 = bf16[1,4,128,1024]{3,2,0,1:T(8,128)(2,1)} async-done(((bf16[1,4,128,1024]{3,2,0,1:T(8,128)(2,1)}), bf16[1,4,128,1024]{3,2,0,1:T(8,128)(2,1)}, u32[]{:S(2)}, u32[]{:S(2)}) %all-to-all-start.1) | async-done | bytes 1048608 | tf_op jit(solution)/shard_map/all_to_all | solution.py:73
  100.2 4.4 all-to-all-start.2
  110.9 18.8 %all-to-all-done.2 = bf16[1,4,128,1024]{3,2,0,1:T(8,128)(2,1)} async-done(((bf16[1,4,128,1024]{3,2,0,1:T(8,128)(2,1)}), bf16[1,4,128,1024]{3,2,0,1:T(8,128)(2,1)}, u32[]{:S(2)}, u32[]{:S(2)}) %all-to-all-start.2) | async-done | bytes 1048608 | tf_op jit(solution)/shard_map/all_to_all | solution.py:74
  132.5 78.6 %while.17 = (s32[]{:T(128)}, bf16[8,1,512,128]{3,2,1,0:T(8,128)(2,1)}, bf16[8,1,512,128]{3,2,1,0:T(8,128)(2,1)}, bf16[8,1,512,128]{3,2,1,0:T(8,128)(2,1)}, bf16[...) while((s32[]{:T(128)}, ...), condition=%wide.region_5.6_spmd.clone, body=%wide.region_1.5_spmd.clone.sunk | while | flops 408418816 | bytes 12093549 | solution.py:88
  134.0 1.9 fusion.107
  138.4 1.9 fusion.105
  140.3 1.9 fusion.104
  148.3 1.9 fusion.105
  150.2 1.9 fusion.104
  158.1 1.9 fusion.105
  160.0 1.9 fusion.104
  167.9 1.9 fusion.105
  169.8 1.9 fusion.104
  177.7 1.9 fusion.105
  179.7 1.9 fusion.104
  187.6 1.9 fusion.105
  189.5 1.9 fusion.104
  197.4 1.9 fusion.105
  199.3 1.9 fusion.104
  207.2 1.9 fusion.105
  209.1 1.9 fusion.104
  211.1 1.9 copy.67
  214.3 4.2 all-to-all-start.4
  218.5 1.9 copy.71
  221.7 22.1 %all-to-all-done.4 = bf16[1,4,128,1024]{3,2,0,1:T(8,128)(2,1)} async-done(((bf16[1,4,128,1024]{3,2,0,1:T(8,128)(2,1)}), bf16[1,4,128,1024]{3,2,0,1:T(8,128)(2,1)}, u32[]{:S(2)}, u32[]{:S(2)}) %all-to-all-start.4) | async-done | bytes 1048608 | tf_op jit(solution)/shard_map/all_to_all | solution.py:98
  243.8 4.3 all-to-all-start.5
  248.1 1.9 copy.75
  251.2 22.1 %all-to-all-done.5 = bf16[1,4,128,1024]{3,2,0,1:T(8,128)(2,1)} async-done(((bf16[1,4,128,1024]{3,2,0,1:T(8,128)(2,1)}), bf16[1,4,128,1024]{3,2,0,1:T(8,128)(2,1)}, u32[]{:S(2)}, u32[]{:S(2)}) %all-to-all-start.5) | async-done | bytes 1048608 | tf_op jit(solution)/shard_map/all_to_all | solution.py:99
  273.3 4.2 all-to-all-start.6
  277.6 1.9 copy.79
  280.8 2.2 convolution_convert_fusion.8
  283.3 5.6 %fusion.41 = f32[1024,2048]{1,0:T(8,128)} fusion(bf16[512,1024]{1,0:T(8,128)(2,1)S(1)} %bitcast.215, bf16[1,1,512,2048]{3,2,1,0:T(8,128)(2,1)S(1)} %copy-done), kind=kOutput, calls=%fused_computation.47 | convolution fusion | flops 2147483648 | bytes 11534336 | tf_op jit(solution)/shard_map/svtf,svtd->fd/dot_general | solution.py:110
  288.9 14.0 %all-to-all-done.6 = bf16[1,4,128,1024]{3,2,0,1:T(8,128)(2,1)} async-done(((bf16[1,4,128,1024]{3,2,0,1:T(8,128)(2,1)}), bf16[1,4,128,1024]{3,2,0,1:T(8,128)(2,1)}, u32[]{:S(2)}, u32[]{:S(2)}) %all-to-all-start.6) | async-done | bytes 1048608 | tf_op jit(solution)/shard_map/all_to_all | solution.py:100
  302.9 4.2 all-to-all-start.7
  307.1 147.3 %all-reduce.1 = bf16[1024,2048]{1,0:T(8,128)(2,1)} all-reduce(f32[1024,2048]{1,0:T(8,128)} %fusion.41), channel_id=1, replica_groups=mesh['scene'=64,'view'=4] {'scene','view'}, use_global_device_ids=true, to_apply=%region_6.7 | all-reduce | flops 2097152 | bytes 12582912 | tf_op jit(solution)/shard_map/psum | solution.py:113
  454.4 2.2 convolution_convert_fusion.7
  457.9 2.3 convolution_convert_fusion.6
  461.5 3.7 fusion.40
  465.2 2.2 convolution_convert_fusion.5
  (99 shorter events, 72.0 us)
Async XLA Ops:
  0.6 1.6 copy-start
  9.4 31.7 %all-to-all-start.3 = ((bf16[1,4,128,1024]{3,2,0,1:T(8,128)(2,1)}), bf16[1,4,128,1024]{3,2,0,1:T(8,128)(2,1)S(1)}, u32[]{:S(2)}, u32[]{:S(2)}) async-start(bf16[1,4,128,1024]{3,2,0,1:T(8,128)(2,1)} %copy.61), calls=%async_computation.3 | async-start | bytes 2097152 | tf_op jit(solution)/shard_map/all_to_all | solution.py:75
  41.1 29.5 %all-to-all-start = ((bf16[1,4,128,1024]{3,2,0,1:T(8,128)(2,1)}), bf16[1,4,128,1024]{3,2,0,1:T(8,128)(2,1)}, u32[]{:S(2)}, u32[]{:S(2)}) async-start(bf16[1,4,128,1024]{3,2,0,1:T(8,128)(2,1)} %copy.52), calls=%async_computation | async-start | bytes 2097152 | tf_op jit(solution)/shard_map/all_to_all | solution.py:72
  70.6 29.5 %all-to-all-start.1 = ((bf16[1,4,128,1024]{3,2,0,1:T(8,128)(2,1)}), bf16[1,4,128,1024]{3,2,0,1:T(8,128)(2,1)}, u32[]{:S(2)}, u32[]{:S(2)}) async-start(bf16[1,4,128,1024]{3,2,0,1:T(8,128)(2,1)} %copy.55), calls=%async_computation.1 | async-start | bytes 2097152 | tf_op jit(solution)/shard_map/all_to_all | solution.py:73
  77.3 27.4 %copy-start.1 = (s32[1,4,4]{2,1,0:T(4,128)S(1)}, s32[1,4,4]{2,1,0:T(4,128)}, u32[]{:S(2)}) copy-start(s32[1,4,4]{2,1,0:T(4,128)} %param.14) | copy-start | bytes 196
  77.3 27.5 %copy-start.2 = (s32[1,4,4]{2,1,0:T(4,128)S(1)}, s32[1,4,4]{2,1,0:T(4,128)}, u32[]{:S(2)}) copy-start(s32[1,4,4]{2,1,0:T(4,128)} %param.15) | copy-start | bytes 196
  100.2 29.5 %all-to-all-start.2 = ((bf16[1,4,128,1024]{3,2,0,1:T(8,128)(2,1)}), bf16[1,4,128,1024]{3,2,0,1:T(8,128)(2,1)}, u32[]{:S(2)}, u32[]{:S(2)}) async-start(bf16[1,4,128,1024]{3,2,0,1:T(8,128)(2,1)} %copy.58), calls=%async_computation.2 | async-start | bytes 2097152 | tf_op jit(solution)/shard_map/all_to_all | solution.py:74
  214.3 29.5 %all-to-all-start.4 = ((bf16[1,4,128,1024]{3,2,0,1:T(8,128)(2,1)}), bf16[1,4,128,1024]{3,2,0,1:T(8,128)(2,1)}, u32[]{:S(2)}, u32[]{:S(2)}) async-start(bf16[1,4,128,1024]{3,2,0,1:T(8,128)(2,1)} %bitcast.21), calls=%async_computation.4 | async-start | bytes 2097152 | tf_op jit(solution)/shard_map/all_to_all | solution.py:98
  243.8 29.5 %all-to-all-start.5 = ((bf16[1,4,128,1024]{3,2,0,1:T(8,128)(2,1)}), bf16[1,4,128,1024]{3,2,0,1:T(8,128)(2,1)}, u32[]{:S(2)}, u32[]{:S(2)}) async-start(bf16[1,4,128,1024]{3,2,0,1:T(8,128)(2,1)} %bitcast.26), calls=%async_computation.5 | async-start | bytes 2097152 | tf_op jit(solution)/shard_map/all_to_all | solution.py:99
  273.3 29.5 %all-to-all-start.6 = ((bf16[1,4,128,1024]{3,2,0,1:T(8,128)(2,1)}), bf16[1,4,128,1024]{3,2,0,1:T(8,128)(2,1)}, u32[]{:S(2)}, u32[]{:S(2)}) async-start(bf16[1,4,128,1024]{3,2,0,1:T(8,128)(2,1)} %bitcast.30), calls=%async_computation.6 | async-start | bytes 2097152 | tf_op jit(solution)/shard_map/all_to_all | solution.py:100
  302.9 162.4 %all-to-all-start.7 = ((bf16[1,4,128,1024]{3,2,0,1:T(8,128)(2,1)}), bf16[1,4,128,1024]{3,2,0,1:T(8,128)(2,1)}, u32[]{:S(2)}, u32[]{:S(2)}) async-start(bf16[1,4,128,1024]{3,2,0,1:T(8,128)(2,1)} %bitcast.34), calls=%async_computation.7 | async-start | bytes 2097152 | tf_op jit(solution)/shard_map/all_to_all | solution.py:101
  457.9 3.6 copy-start.3
where the time goes:
time: 471 us; the launch traced here: 469 us
  blocking collectives  147 us (31%)
  waiting for transfers between devices  142 us (30%)
  matrix products  105 us (22%)
  starting transfers between devices  36.4 us (8%)
  local copies, waits for them, and re-layouts  33 us (7%)
    psum x1, blocking collectives, body(): grad_w_out = lax.psum(partial_grad, ('scene', 'view')).astype(jnp.bfloat16)  147 us
    all_to_all x1, waiting for transfers between devices, body(): lax.all_to_all(join_heads(results[0]), 'view', split_axis=1, concat_axis=...  22.1 us
    all_to_all x1, waiting for transfers between devices, body(): lax.all_to_all(join_heads(results[1]), 'view', split_axis=1, concat_axis=...  22.1 us
    all_to_all x1, waiting for transfers between devices, body(): lax.all_to_all(pack(queries), 'view', split_axis=1, concat_axis=1, tiled=...  21.6 us
    all_to_all x1, waiting for transfers between devices, body(): lax.all_to_all(pack(keys), 'view', split_axis=1, concat_axis=1, tiled=True)  21.6 us
    all_to_all x1, waiting for transfers between devices, body(): lax.all_to_all(pack(grad_attn), 'view', split_axis=1, concat_axis=1, tile...  21.6 us
    all_to_all x1, waiting for transfers between devices, body(): lax.all_to_all(pack(values), 'view', split_axis=1, concat_axis=1, tiled=T...  18.8 us
    dot_general x8, matrix products, head_pass(): jnp.einsum('sij,sjd->sid', weights_b, values_h, preferred_element_type=jn...  15.5 us
  transfers between devices with their start and end apart: 8, of which 7 were waited for; matrix products, arithmetic and copies ran while one was open for 10% of the time, Pallas kernels for 0%

commit v1 on v0

v1 whole, which is shorter than its diff:
```python
import functools
import math

import jax
import jax.numpy as jnp
from jax import lax
from jax.experimental import pallas as pl
from jax.experimental.pallas import tpu as pltpu
from jax.sharding import PartitionSpec as P

HDIM = 128
BLK = 128
NEG_FILL = -1e30
MESH = pl.DeviceIdType.MESH
F32 = jnp.float32
BF16 = jnp.bfloat16
REDUCE = True
TIMING = False
PINNED = True
NT = (((1,), (1,)), ((), ()))
TN = (((0,), (0,)), ((), ()))


def dot(a, b, dims=(((1,), (0,)), ((), ()))):
    return lax.dot_general(a, b, dims, preferred_element_type=F32)


def place(core, y, x, z_hi):
    return ((z_hi * 4 + y) * 4 + x) * 2 + core


def kernel(
    heads,
    views,
    q_hbm, k_hbm, v_hbm, og_hbm, w_hbm, bucket_ref, pair_ref,
    lo_ref, gq_ref, gk_ref, gv_ref, gw_ref,
    qkv_in, og, w, snd, rcv, ga_buf, ga_snd, ga_rcv, mask, wts, gs, gs_t,
    att_snd, att_rcv, att, att_t, g_snd, g_rcv,
    load_sem, big_sem, qs_sem, qr_sem, as_sem, ar_sem, gs_sem, gr_sem, bs_sem, br_sem,
    *reduce_refs,
):
    scene = lax.axis_index("scene")
    me = lax.axis_index("view")
    rows = views * BLK
    inv_root = 1.0 / math.sqrt(HDIM)
    offsets = range(1, views)
    at = [lax.rem(me + o, views) for o in range(views)]
    came = [lax.rem(me + views - o, views) for o in range(views)]

    peers = [(scene, at[o]) for o in offsets]
    if REDUCE:
        part, gsum, r0, r1, r2, zsrc, rz, zg, cs, cr, s1s, s1r, s2s, s2r, zs, zr, ts, tr, g2s, g2r, g1s, g1r, gcs, gcr = reduce_refs
        core = lax.rem(scene, 2)
        x = lax.rem(scene // 2, 4)
        y = lax.rem(scene // 8, 4)
        z_hi = scene // 32
        z = z_hi * 4 + me
        first_x = 1 - core
        i1 = first_x * x + core * y
        i2 = first_x * y + core * x
        other = (place(1 - core, y, x, z_hi), me)
        axis1, axis2, along_z = [], [], []
        for o in range(1, 4):
            x1, y1 = lax.rem(x + o * first_x, 4), lax.rem(y + o * core, 4)
            x2, y2 = lax.rem(x + o * core, 4), lax.rem(y + o * first_x, 4)
            axis1.append((place(core, y1, x1, z_hi), me))
            axis2.append((place(core, y2, x2, z_hi), me))
        for o in range(1, 8):
            zz = lax.rem(z + o, 8)
            along_z.append((place(core, y, x, zz // 4), lax.rem(zz, 4)))
        peers = [other] + axis1 + axis2 + along_z

    barrier = pltpu.get_barrier_semaphore()
    for peer in peers:
        pl.semaphore_signal(barrier, inc=1, device_id=peer, device_id_type=MESH)

    loads = []
    for part_id, cols in enumerate((pl.ds(0, 2 * HDIM), pl.ds(2 * HDIM, (heads - 2) * HDIM))):
        for t, ref in enumerate((q_hbm, k_hbm, v_hbm)):
            copy = pltpu.make_async_copy(
                ref.at[:, :, cols], qkv_in.at[t, :, :, cols], load_sem.at[t, part_id]
            )
            copy.start()
            loads.append(copy)
    w_load = pltpu.make_async_copy(w_hbm, w, big_sem.at[0])
    og_load = pltpu.make_async_copy(og_hbm, og, big_sem.at[1])
    og_load.start()
    w_load.start()

    block_at = []
    for o in range(views):
        found = jnp.int32(0)
        for j in range(views):
            found = jnp.where(bucket_ref[me, j] == at[o], j, found)
        block_at.append(found)
    lane_view = lax.broadcasted_iota(jnp.int32, (1, rows), 1) // BLK
    for a in range(views):
        row = jnp.zeros((1, rows), F32)
        for b in range(views):
            live = jnp.int32(0)
            for j in range(views):
                live = live + jnp.where(bucket_ref[b, j] == me, 1, 0)
            ok = jnp.where((pair_ref[a, b] > 0) & (live > 0), 1.0, 0.0)
            row = row + jnp.where(lane_view == b, ok, 0.0)
        mask[a] = row

    def cols_of(h, n=1):
        return pl.ds(pl.multiple_of(h * HDIM, HDIM), n * HDIM)

    def qkv_copy(h, o, to):
        slot = at[o] if to else came[o]
        return pltpu.make_async_remote_copy(
            src_ref=snd.at[h, :, at[o]],
            dst_ref=rcv.at[h, :, me if to else slot],
            send_sem=qs_sem.at[h, o],
            recv_sem=qr_sem.at[h, o],
            device_id=(scene, at[o]),
            device_id_type=MESH,
        )

    def ga_copy(h, o, to):
        return pltpu.make_async_remote_copy(
            src_ref=ga_snd.at[h, at[o]],
            dst_ref=ga_rcv.at[h, me if to else came[o]],
            send_sem=as_sem.at[h, o],
            recv_sem=ar_sem.at[h, o],
            device_id=(scene, at[o]),
            device_id_type=MESH,
        )

    def att_copy(h, o, to):
        return pltpu.make_async_remote_copy(
            src_ref=att_snd.at[h, at[o]],
            dst_ref=att_rcv.at[h, me if to else came[o]],
            send_sem=bs_sem.at[h, o],
            recv_sem=br_sem.at[h, o],
            device_id=(scene, at[o]),
            device_id_type=MESH,
        )

    def grad_copy(h, o, to):
        return pltpu.make_async_remote_copy(
            src_ref=g_snd.at[h, :, at[o]],
            dst_ref=g_rcv.at[h, :, me if to else came[o]],
            send_sem=gs_sem.at[h, o],
            recv_sem=gr_sem.at[h, o],
            device_id=(scene, at[o]),
            device_id_type=MESH,
        )

    def pick(which, blocks):
        block = blocks[0]
        for j in range(1, views):
            block = lax.select_n(which == j, block, blocks[j])
        return block

    def send_qkv(h, carry):
        for t in range(3):
            blocks = [qkv_in[t, j, :, cols_of(h)] for j in range(views)]
            for o in range(views):
                block = pick(block_at[o], blocks)
                if o == 0:
                    rcv[h, t, me] = block
                else:
                    snd[h, t, at[o]] = block
        for o in offsets:
            qkv_copy(h, o, True).start()
        return carry

    for copy in loads[:3]:
        copy.wait()
    pl.semaphore_wait(barrier, len(peers))
    lax.fori_loop(0, 2, send_qkv, 0)
    for copy in loads[3:]:
        copy.wait()
    lax.fori_loop(2, heads, send_qkv, 0)

    og_load.wait()
    w_load.wait()

    def make_ga(p, carry):
        ga = dot(og[...], w[pl.ds(pl.multiple_of(p * 2 * HDIM, 2 * HDIM), 2 * HDIM), :], NT)
        ga_buf[:, :, cols_of(2 * p, 2)] = ga.astype(BF16).reshape(views, BLK, 2 * HDIM)
        for s in range(2):
            h = 2 * p + s
            for o in range(views):
                block = ga_buf[block_at[o], :, cols_of(h)]
                if o == 0:
                    ga_rcv[h, me] = block
                else:
                    ga_snd[h, at[o]] = block
        return carry

    lax.fori_loop(0, heads // 2, make_ga, 0)

    def forward(h, carry):
        for o in offsets:
            qkv_copy(h, o, False).wait_recv()
        keys = rcv[h, 1].reshape(rows, HDIM)
        values = rcv[h, 2].reshape(rows, HDIM)
        for o in (1, 2, 3, 0):
            a = at[o]
            scores = dot(rcv[h, 0, a], keys, NT) * inv_root
            scores = jnp.where(mask[a] > 0.5, scores, NEG_FILL)
            peak = jnp.max(scores, axis=1, keepdims=True)
            exponent = jnp.exp(scores - peak)
            weights = exponent * (1.0 / jnp.sum(exponent, axis=1, keepdims=True))
            wts[h, a] = weights
            attended = dot(weights.astype(BF16), values).astype(BF16)
            if o == 0:
                att_rcv[h, me] = attended
            else:
                att_snd[h, a] = attended
                att_copy(h, o, True).start()
        return carry

    lax.fori_loop(0, heads, forward, 0)

    def send_ga(h, carry):
        for o in offsets:
            ga_copy(h, o, True).start()
        return carry

    lax.fori_loop(0, heads, send_ga, 0)

    def backward(h, carry):
        for o in offsets:
            ga_copy(h, o, False).wait_recv()
        keys = rcv[h, 1].reshape(rows, HDIM)
        values = rcv[h, 2].reshape(rows, HDIM)
        for a in range(views):
            weights = wts[h, a]
            grad_weights = dot(ga_rcv[h, a], values, NT)
            row_dot = jnp.sum(weights * grad_weights, axis=1, keepdims=True)
            grad_scores = (weights * (grad_weights - row_dot) * inv_root).astype(BF16)
            gs[pl.ds(a * BLK, BLK), :] = grad_scores
            gs_t[pl.ds(a * BLK, BLK), :] = weights.astype(BF16)
            g_snd[h, 0, a] = dot(grad_scores, keys).astype(BF16)
        queries = rcv[h, 0].reshape(rows, HDIM)
        grads = ga_rcv[h].reshape(rows, HDIM)
        grad_keys = dot(queries, gs[...], TN).T
        g_snd[h, 1] = grad_keys.astype(BF16).reshape(views, BLK, HDIM)
        grad_values = dot(grads, gs_t[...], TN).T
        g_snd[h, 2] = grad_values.astype(BF16).reshape(views, BLK, HDIM)
        for o in offsets:
            grad_copy(h, o, True).start()
        g_rcv[h, :, me] = g_snd[h, :, me]
        return carry

    home = [bucket_ref[me, j] for j in range(views)]

    def unpack_att(h, carry):
        for o in offsets:
            att_copy(h, o, False).wait_recv()
        blocks = [att_rcv[h, b] for b in range(views)]
        for j in range(views):
            block = pick(home[j], blocks)
            att[pl.ds(j * BLK, BLK), cols_of(h)] = block
            att_t[cols_of(h), pl.ds(j * BLK, BLK)] = block.T
        return carry

    width = heads * HDIM
    wide = 256

    def make_out(c, carry):
        cols = pl.ds(pl.multiple_of(c * wide, wide), wide)
        lo_ref[:, cols] = dot(att[...], w[:, cols]).astype(BF16)
        return carry

    def make_part(c, carry):
        span = pl.ds(pl.multiple_of(c * wide, wide), wide)
        for d in range(og.shape[1] // 512):
            cols = pl.ds(d * 512, 512)
            term = dot(att_t[span, :], og[:, cols])
            if REDUCE:
                part[span, cols] = term.astype(BF16)
            else:
                gw_ref[span, cols] = term
        return carry

    lax.fori_loop(0, heads, unpack_att, 0)
    lax.fori_loop(0, width // wide, make_part, 0)
    if REDUCE:
        half = width // 2
        core_rows = pl.ds(pl.multiple_of(core * half, half), half)
        other_rows = pl.ds(pl.multiple_of((1 - core) * half, half), half)

        def remote(src, dst, s_sem, r_sem, to):
            return pltpu.make_async_remote_copy(
                src_ref=src, dst_ref=dst, send_sem=s_sem, recv_sem=r_sem,
                device_id=to, device_id_type=MESH,
            )

        c_copy = remote(part.at[other_rows], r0, cs, cr, other)
        c_copy.start()
    lax.fori_loop(0, lo_ref.shape[1] // wide, make_out, 0)

    if not REDUCE:
        lax.fori_loop(0, heads, backward, 0)
    else:
        lax.fori_loop(0, 1, backward, 0)
        c_copy.wait()

        def sum_core(i, carry):
            piece = pl.ds(pl.multiple_of(i * 32, 32), 32)
            mine = pl.ds(pl.multiple_of(core * half + i * 32, 32), 32)
            gsum[piece] = (part[mine].astype(F32) + r0[piece].astype(F32)).astype(BF16)
            return carry

        lax.fori_loop(0, half // 32, sum_core, 0)

        def rows_of(i, n):
            return pl.ds(pl.multiple_of(i * n, n), n)

        rs1 = [
            remote(gsum.at[rows_of(lax.rem(i1 + o, 4), 128)], r1.at[o - 1], s1s.at[o - 1], s1r.at[o - 1], axis1[o - 1])
            for o in range(1, 4)
        ]
        for copy in rs1:
            copy.start()
        lax.fori_loop(1, 2, backward, 0)
        for copy in rs1:
            copy.wait()

        def sum_1(i, carry):
            piece = pl.ds(pl.multiple_of(i * 32, 32), 32)
            total = gsum[pl.ds(pl.multiple_of(i1 * 128 + i * 32, 32), 32)].astype(F32)
            for o in range(3):
                total = total + r1[o, piece].astype(F32)
            r0[piece] = total.astype(BF16)
            return carry

        lax.fori_loop(0, 4, sum_1, 0)
        rs2 = [
            remote(r0.at[rows_of(lax.rem(i2 + o, 4), 32)], r2.at[o - 1], s2s.at[o - 1], s2r.at[o - 1], axis2[o - 1])
            for o in range(1, 4)
        ]
        for copy in rs2:
            copy.start()
        for copy in rs2:
            copy.wait()
        total = r0[rows_of(i2, 32)].astype(F32)
        for o in range(3):
            total = total + r2[o].astype(F32)
        total = total.astype(BF16)
        for p in range(8):
            zsrc[p] = total[:, p * 256:(p + 1) * 256]
        rsz = [
            remote(zsrc.at[lax.rem(z + o, 8)], rz.at[o - 1], zs.at[o - 1], zr.at[o - 1], along_z[o - 1])
            for o in range(1, 8)
        ]
        for copy in rsz:
            copy.start()
        lax.fori_loop(2, 3, backward, 0)
        for copy in rsz:
            copy.wait()
        total = zsrc[z].astype(F32)
        for o in range(7):
            total = total + rz[o].astype(F32)
        zg[z] = total.astype(BF16)
        agz = [
            remote(zg.at[z], zg.at[z], ts.at[o - 1], tr.at[o - 1], along_z[o - 1])
            for o in range(1, 8)
        ]
        for copy in agz:
            copy.start()
        lax.fori_loop(3, 4, backward, 0)
        for o in range(1, 8):
            src = zg.at[lax.rem(z + 8 - o, 8)]
            remote(src, src, ts.at[o - 1], tr.at[o - 1], along_z[o - 1]).wait()
        for p in range(8):
            gw_ref[core, i1, i2, :, pl.ds(p * 256, 256)] = zg[p]
        ag2 = []
        for o in range(1, 4):
            spot = gw_ref.at[core, i1, i2]
            remote(spot, spot, g2s.at[o - 1], g2r.at[o - 1], axis2[o - 1]).start()
        lax.fori_loop(4, 5, backward, 0)
        for o in range(1, 4):
            spot = gw_ref.at[core, i1, lax.rem(i2 + 4 - o, 4)]
            remote(spot, spot, g2s.at[o - 1], g2r.at[o - 1], axis2[o - 1]).wait()
        for o in range(1, 4):
            spot = gw_ref.at[core, i1]
            remote(spot, spot, g1s.at[o - 1], g1r.at[o - 1], axis1[o - 1]).start()
        lax.fori_loop(5, heads, backward, 0)
        for o in range(1, 4):
            spot = gw_ref.at[core, lax.rem(i1 + 4 - o, 4)]
            remote(spot, spot, g1s.at[o - 1], g1r.at[o - 1], axis1[o - 1]).wait()
        spot = gw_ref.at[core]
        remote(spot, spot, gcs, gcr, other).start()

    def finish(h, carry):
        for o in offsets:
            grad_copy(h, o, False).wait_recv()
        for t, ref in enumerate((gq_ref, gk_ref, gv_ref)):
            blocks = [g_rcv[h, t, b] for b in range(views)]
            for j in range(views):
                ref[j, :, cols_of(h)] = pick(home[j], blocks)
        for o in offsets:
            qkv_copy(h, o, True).wait_send()
            ga_copy(h, o, True).wait_send()
            att_copy(h, o, True).wait_send()
            grad_copy(h, o, True).wait_send()
        return carry

    lax.fori_loop(0, heads, finish, 0)
    if REDUCE:
        spot = gw_ref.at[1 - core]
        remote(spot, spot, gcs, gcr, other).wait()


def write_out(*refs):
    count = (len(refs) - 1) // 2
    sems = refs[-1]
    copies = [
        pltpu.make_async_copy(refs[i], refs[count + i], sems.at[i]) for i in range(count)
    ]
    for copy in copies:
        copy.start()
    for copy in copies:
        copy.wait()


def body(queries, keys, values, out_grad, w_out, bucket_of, pair_mask):
    views = lax.axis_size("view")
    tokens, width = queries.shape[2:]
    heads = width // HDIM
    model = out_grad.shape[-1]
    rows = views * BLK
    blocks = (views, BLK, width)
    vmem = pl.BlockSpec(memory_space=pltpu.VMEM)
    smem = pl.BlockSpec(memory_space=pltpu.SMEM)
    hbm = pl.BlockSpec(memory_space=pl.ANY)
    dma = pltpu.SemaphoreType.DMA
    scratch = [
        pltpu.VMEM((3,) + blocks, BF16),
        pltpu.VMEM((tokens, model), BF16),
        pltpu.VMEM((width, model), BF16),
        pltpu.VMEM((heads, 3, views, BLK, HDIM), BF16),
        pltpu.VMEM((heads, 3, views, BLK, HDIM), BF16),
        pltpu.VMEM(blocks, BF16),
        pltpu.VMEM((heads, views, BLK, HDIM), BF16),
        pltpu.VMEM((heads, views, BLK, HDIM), BF16),
        pltpu.VMEM((views, 1, rows), F32),
        pltpu.VMEM((heads, views, BLK, rows), F32),
        pltpu.VMEM((rows, rows), BF16),
        pltpu.VMEM((rows, rows), BF16),
        pltpu.VMEM((heads, views, BLK, HDIM), BF16),
        pltpu.VMEM((heads, views, BLK, HDIM), BF16),
        pltpu.VMEM((tokens, width), BF16),
        pltpu.VMEM((width, tokens), BF16),
        pltpu.VMEM((heads, 3, views, BLK, HDIM), BF16),
        pltpu.VMEM((heads, 3, views, BLK, HDIM), BF16),
        dma((3, 2)),
        dma((2,)),
    ] + [dma((heads, views))] * 8
    if REDUCE:
        scratch += [
            pltpu.VMEM((width, model), BF16),
            pltpu.VMEM((width // 2, model), BF16),
            pltpu.VMEM((width // 2, model), BF16),
            pltpu.VMEM((3, 128, model), BF16),
            pltpu.VMEM((3, 32, model), BF16),
            pltpu.VMEM((8, 32, model // 8), BF16),
            pltpu.VMEM((7, 32, model // 8), BF16),
            pltpu.VMEM((8, 32, model // 8), BF16),
            dma, dma,
            dma((3,)), dma((3,)), dma((3,)), dma((3,)),
            dma((7,)), dma((7,)), dma((7,)), dma((7,)),
            dma((3,)), dma((3,)), dma((3,)), dma((3,)),
            dma, dma,
        ]
        gw_shape = jax.ShapeDtypeStruct((2, 4, 4, 32, model), BF16)
    else:
        gw_shape = jax.ShapeDtypeStruct((width, model), F32)
    grad_shape = jax.ShapeDtypeStruct(blocks, BF16)
    shapes = (
        jax.ShapeDtypeStruct((tokens, model), BF16),
        grad_shape, grad_shape, grad_shape, gw_shape,
    )
    done = pl.pallas_call(
        functools.partial(kernel, heads, views),
        out_shape=tuple(pltpu.VMEM(s.shape, s.dtype) for s in shapes) if PINNED else shapes,
        in_specs=[hbm] * 5 + [smem] * 2,
        out_specs=[vmem] * 5,
        scratch_shapes=scratch,
        compiler_params=pltpu.CompilerParams(
            collective_id=0, has_side_effects=True, vmem_limit_bytes=51 * 1024 * 1024
        ),
        cost_estimate=pl.CostEstimate(
            flops=9_700_000_000, bytes_accessed=18_000_000, transcendentals=2_100_000
        ),
    )(
        queries.reshape(blocks), keys.reshape(blocks), values.reshape(blocks),
        out_grad.reshape(tokens, model), w_out,
        bucket_of.reshape(views, views), pair_mask.reshape(views, views),
    )
    if PINNED:
        done = [pltpu.with_memory_space_constraint(d, pltpu.VMEM) for d in done]
    layer_out, grad_q, grad_k, grad_v, grad_w = pl.pallas_call(
        write_out,
        out_shape=shapes,
        in_specs=[vmem] * 5,
        out_specs=[hbm] * 5,
        scratch_shapes=[dma((5,))],
        compiler_params=pltpu.CompilerParams(vmem_limit_bytes=1024 * 1024),
    )(*done)
    if REDUCE or TIMING:
        grad_w = grad_w.reshape(width, model).astype(BF16)
    else:
        grad_w = lax.psum(grad_w, ("scene", "view")).astype(BF16)
    shape = queries.shape
    return (
        layer_out.reshape(1, 1, tokens, model),
        grad_q.reshape(shape), grad_k.reshape(shape), grad_v.reshape(shape), grad_w,
    )


def solution(mesh):
    split = P("scene", "view", None, None)
    return jax.shard_map(
        body,
        mesh=mesh,
        in_specs=(split, split, split, split, P(), P("scene", None, None), P("scene", None, None)),
        out_specs=(split, split, split, split, P()),
        check_vma=False,
    )
```

time: 471 us -> 207 us (0.44)
  Pallas kernels: 0 us -> 204 us
  blocking collectives: 147 us -> 0 us
  waiting for transfers between devices: 142 us -> 0 us
  matrix products: 105 us -> 0 us
  starting transfers between devices: 36.4 us -> 0 us
  local copies, waits for them, and re-layouts: 33 us -> 0 us
    pallas_call x0 -> x2, Pallas kernels: none -> 204 us  [the longest x1 201 us: body(): pl.pallas_call(functools.partial(kernel, heads, views), out_shape=tuple((...]
    psum x1 -> x0, blocking collectives: 147 us -> none  [body(): grad_w_out = lax.psum(partial_grad, ('scene', 'view')).astype(jnp.bfloat16)]
    all_to_all x8 -> x0, waiting for transfers between devices: 142 us -> none  [the longest x1 22.1 us: body(): lax.all_to_all(join_heads(results[0]), 'view', split_axis=1, concat_axis=...]
    dot_general x59 -> x0, matrix products: 105 us -> none  [the longest x8 15.5 us: head_pass(): jnp.einsum('sij,sjd->sid', weights_b, values_h, preferred_element_type=jn...]
    all_to_all x8 -> x0, starting transfers between devices: 36.4 us -> none  [the longest x1 6.45 us: body(): lax.all_to_all(pack(grad_attn), 'view', split_axis=1, concat_axis=1, tile...]
    convert_element_type x8 -> x0, local copies, waits for them, and re-layouts: 9.29 us -> none  [the longest x4 5.13 us: pack(): return jnp.einsum('sdb,sbrf->sdrf', selector, blocks, preferred_element_t...]
    unnamed x18 -> x0, local copies, waits for them, and re-layouts: 9.21 us -> none
    transpose x8 -> x0, local copies, waits for them, and re-layouts: 7.9 us -> none  [the longest x4 7.62 us: join_heads(): tensor.transpose(1, 2, 0, 3).reshape(scenes_here, view_count, BLK, width)]
  transfers between devices with their start and end apart: 8 -> 0, of which waited for: 7 -> 0; matrix products, arithmetic and copies ran while one was open for 10% -> 0% of each run, Pallas kernels for 0% -> 0%
where the time goes in v1:
time: 207 us; the launch traced here: 205 us
  Pallas kernels  204 us (99%)
    pallas_call x1, Pallas kernels, body(): pl.pallas_call(functools.partial(kernel, heads, views), out_shape=tuple((...  201 us

profile of v1, /device:TPU:1, one launch (start us, length us, event | category | flops | bytes accessed | tf_op | source)
XLA Modules:
  0.0 205.0 jit_solution(242803402737859045)
XLA Ops:
  0.6 200.6 %shard_map.110 = (bf16[512,2048]{1,0:T(8,128)(2,1)S(1)}, bf16[4,128,1024]{2,1,0:T(8,128)(2,1)S(1)}, bf16[4,128,1024]{2,1,0:T(8,128)(2,1)S(1)}, bf16[4,128,1024]{...) custom-call(bf16[4,128,1024]{2,1,0:T(8,128)(2,1)} %bitcast.14, bf16[4,128,1024]{2,1,0:T(8,128)(2,1)} %bitcast.15, ...), custom_call_target="tpu_custom_call" | custom-call | flops 9699999744 | bytes 18000000 | tf_op jit(solution)/shard_map/pallas_call | solution.py:480
  201.2 3.8 %shard_map.111 = (bf16[512,2048]{1,0:T(8,128)(2,1)}, bf16[4,128,1024]{2,1,0:T(8,128)(2,1)}, bf16[4,128,1024]{2,1,0:T(8,128)(2,1)}, bf16[4,128,1024]{2,1,0:T(8,128)(2,1)}, bf16[2,4,4,32,2048]{4,3,2,1,0:T(8,128)(2,1)}) custom-call(bf16[512,2048]{1,0:T(8,128)(2,1)S(1)} %get-tuple-element.15.refs_0_, bf16[4,128,1024]{2,1,0:T(8,128)(2,1)S(1)} %get-tuple-element.16.refs_1_, ...), custom_call_target="tpu_custom_call" | custom-call | tf_op jit(solution)/shard_map/pallas_call | solution.py:499

commit v2 on v1

--- a/solution.py
+++ b/solution.py
@@ -17,6 +17,7 @@
 REDUCE = True
 TIMING = False
 PINNED = True
+AHEAD = 2
 NT = (((1,), (1,)), ((), ()))
 TN = (((0,), (0,)), ((), ()))
 
@@ -49,7 +50,7 @@
 
     peers = [(scene, at[o]) for o in offsets]
     if REDUCE:
-        part, gsum, r0, r1, r2, zsrc, rz, zg, cs, cr, s1s, s1r, s2s, s2r, zs, zr, ts, tr, g2s, g2r, g1s, g1r, gcs, gcr = reduce_refs
+        part, r0, r1, h1, r2, zsrc, rz, zg, cs, cr, s1s, s1r, s2s, s2r, zs, zr, ts, tr, g2s, g2r, g1s, g1r, gcs, gcr = reduce_refs
         core = lax.rem(scene, 2)
         x = lax.rem(scene // 2, 4)
         y = lax.rem(scene // 8, 4)
@@ -75,7 +76,7 @@
         pl.semaphore_signal(barrier, inc=1, device_id=peer, device_id_type=MESH)
 
     loads = []
-    for part_id, cols in enumerate((pl.ds(0, 2 * HDIM), pl.ds(2 * HDIM, (heads - 2) * HDIM))):
+    for part_id, cols in enumerate((pl.ds(0, HDIM), pl.ds(HDIM, (heads - 1) * HDIM))):
         for t, ref in enumerate((q_hbm, k_hbm, v_hbm)):
             copy = pltpu.make_async_copy(
                 ref.at[:, :, cols], qkv_in.at[t, :, :, cols], load_sem.at[t, part_id]
@@ -154,7 +155,7 @@
             block = lax.select_n(which == j, block, blocks[j])
         return block
 
-    def send_qkv(h, carry):
+    def pack_qkv(h, carry):
         for t in range(3):
             blocks = [qkv_in[t, j, :, cols_of(h)] for j in range(views)]
             for o in range(views):
@@ -163,17 +164,29 @@
                     rcv[h, t, me] = block
                 else:
                     snd[h, t, at[o]] = block
+        return carry
+
+    def start_qkv(h):
         for o in offsets:
             qkv_copy(h, o, True).start()
+
+    def start_ga(h):
+        for o in offsets:
+            ga_copy(h, o, True).start()
+
+    def pack_and_start(h, carry):
+        pack_qkv(h, 0)
+        start_qkv(h)
         return carry
 
     for copy in loads[:3]:
         copy.wait()
     pl.semaphore_wait(barrier, len(peers))
-    lax.fori_loop(0, 2, send_qkv, 0)
+    lax.fori_loop(0, 1, pack_and_start, 0)
     for copy in loads[3:]:
         copy.wait()
-    lax.fori_loop(2, heads, send_qkv, 0)
+    lax.fori_loop(1, AHEAD, pack_and_start, 0)
+    lax.fori_loop(AHEAD, heads, pack_qkv, 0)
 
     og_load.wait()
     w_load.wait()
@@ -193,9 +206,10 @@
 
     lax.fori_loop(0, heads // 2, make_ga, 0)
 
-    def forward(h, carry):
+    def forward(h, more):
         for o in offsets:
             qkv_copy(h, o, False).wait_recv()
+        more()
         keys = rcv[h, 1].reshape(rows, HDIM)
         values = rcv[h, 2].reshape(rows, HDIM)
         for o in (1, 2, 3, 0):
@@ -212,20 +226,12 @@
             else:
                 att_snd[h, a] = attended
                 att_copy(h, o, True).start()
-        return carry
-
-    lax.fori_loop(0, heads, forward, 0)
-
-    def send_ga(h, carry):
-        for o in offsets:
-            ga_copy(h, o, True).start()
-        return carry
-
-    lax.fori_loop(0, heads, send_ga, 0)
-
-    def backward(h, carry):
+
+    def backward(h, more=None):
         for o in offsets:
             ga_copy(h, o, False).wait_recv()
+        if more is not None:
+            more()
         keys = rcv[h, 1].reshape(rows, HDIM)
         values = rcv[h, 2].reshape(rows, HDIM)
         for a in range(views):
@@ -245,7 +251,6 @@
         for o in offsets:
             grad_copy(h, o, True).start()
         g_rcv[h, :, me] = g_snd[h, :, me]
-        return carry
 
     home = [bucket_ref[me, j] for j in range(views)]
 
@@ -267,126 +272,21 @@
         lo_ref[:, cols] = dot(att[...], w[:, cols]).astype(BF16)
         return carry
 
-    def make_part(c, carry):
-        span = pl.ds(pl.multiple_of(c * wide, wide), wide)
-        for d in range(og.shape[1] // 512):
-            cols = pl.ds(d * 512, 512)
-            term = dot(att_t[span, :], og[:, cols])
-            if REDUCE:
-                part[span, cols] = term.astype(BF16)
-            else:
-                gw_ref[span, cols] = term
-        return carry
-
-    lax.fori_loop(0, heads, unpack_att, 0)
-    lax.fori_loop(0, width // wide, make_part, 0)
-    if REDUCE:
-        half = width // 2
-        core_rows = pl.ds(pl.multiple_of(core * half, half), half)
-        other_rows = pl.ds(pl.multiple_of((1 - core) * half, half), half)
-
-        def remote(src, dst, s_sem, r_sem, to):
-            return pltpu.make_async_remote_copy(
-                src_ref=src, dst_ref=dst, send_sem=s_sem, recv_sem=r_sem,
-                device_id=to, device_id_type=MESH,
-            )
-
-        c_copy = remote(part.at[other_rows], r0, cs, cr, other)
-        c_copy.start()
-    lax.fori_loop(0, lo_ref.shape[1] // wide, make_out, 0)
-
-    if not REDUCE:
-        lax.fori_loop(0, heads, backward, 0)
-    else:
-        lax.fori_loop(0, 1, backward, 0)
-        c_copy.wait()
-
-        def sum_core(i, carry):
-            piece = pl.ds(pl.multiple_of(i * 32, 32), 32)
-            mine = pl.ds(pl.multiple_of(core * half + i * 32, 32), 32)
-            gsum[piece] = (part[mine].astype(F32) + r0[piece].astype(F32)).astype(BF16)
+    quarter = width // 4
+
+    def make_part(p):
+        def step(c, carry):
+            rows_in = pl.ds(pl.multiple_of((p * 2 + c) * quarter, quarter), quarter)
+            for d in range(og.shape[1] // 512):
+                cols = pl.ds(d * 512, 512)
+                term = dot(att_t[rows_in, :], og[:, cols])
+                if REDUCE:
+                    part[p, c, :, cols] = term.astype(BF16)
+                else:
+                    gw_ref[rows_in, cols] = term
             return carry
 
-        lax.fori_loop(0, half // 32, sum_core, 0)
-
-        def rows_of(i, n):
-            return pl.ds(pl.multiple_of(i * n, n), n)
-
-        rs1 = [
-            remote(gsum.at[rows_of(lax.rem(i1 + o, 4), 128)], r1.at[o - 1], s1s.at[o - 1], s1r.at[o - 1], axis1[o - 1])
-            for o in range(1, 4)
-        ]
-        for copy in rs1:
-            copy.start()
-        lax.fori_loop(1, 2, backward, 0)
-        for copy in rs1:
-            copy.wait()
-
-        def sum_1(i, carry):
-            piece = pl.ds(pl.multiple_of(i * 32, 32), 32)
-            total = gsum[pl.ds(pl.multiple_of(i1 * 128 + i * 32, 32), 32)].astype(F32)
-            for o in range(3):
-                total = total + r1[o, piece].astype(F32)
-            r0[piece] = total.astype(BF16)
-            return carry
-
-        lax.fori_loop(0, 4, sum_1, 0)
-        rs2 = [
-            remote(r0.at[rows_of(lax.rem(i2 + o, 4), 32)], r2.at[o - 1], s2s.at[o - 1], s2r.at[o - 1], axis2[o - 1])
-            for o in range(1, 4)
-        ]
-        for copy in rs2:
-            copy.start()
-        for copy in rs2:
-            copy.wait()
-        total = r0[rows_of(i2, 32)].astype(F32)
-        for o in range(3):
-            total = total + r2[o].astype(F32)
-        total = total.astype(BF16)
-        for p in range(8):
-            zsrc[p] = total[:, p * 256:(p + 1) * 256]
-        rsz = [
-            remote(zsrc.at[lax.rem(z + o, 8)], rz.at[o - 1], zs.at[o - 1], zr.at[o - 1], along_z[o - 1])
-            for o in range(1, 8)
-        ]
-        for copy in rsz:
-            copy.start()
-        lax.fori_loop(2, 3, backward, 0)
-        for copy in rsz:
-            copy.wait()
-        total = zsrc[z].astype(F32)
-        for o in range(7):
-            total = total + rz[o].astype(F32)
-        zg[z] = total.astype(BF16)
-        agz = [
-            remote(zg.at[z], zg.at[z], ts.at[o - 1], tr.at[o - 1], along_z[o - 1])
-            for o in range(1, 8)
-        ]
-        for copy in agz:
-            copy.start()
-        lax.fori_loop(3, 4, backward, 0)
-        for o in range(1, 8):
-            src = zg.at[lax.rem(z + 8 - o, 8)]
-            remote(src, src, ts.at[o - 1], tr.at[o - 1], along_z[o - 1]).wait()
-        for p in range(8):
-            gw_ref[core, i1, i2, :, pl.ds(p * 256, 256)] = zg[p]
-        ag2 = []
-        for o in range(1, 4):
-            spot = gw_ref.at[core, i1, i2]
-            remote(spot, spot, g2s.at[o - 1], g2r.at[o - 1], axis2[o - 1]).start()
-        lax.fori_loop(4, 5, backward, 0)
-        for o in range(1, 4):
-            spot = gw_ref.at[core, i1, lax.rem(i2 + 4 - o, 4)]
-            remote(spot, spot, g2s.at[o - 1], g2r.at[o - 1], axis2[o - 1]).wait()
-        for o in range(1, 4):
-            spot = gw_ref.at[core, i1]
-            remote(spot, spot, g1s.at[o - 1], g1r.at[o - 1], axis1[o - 1]).start()
-        lax.fori_loop(5, heads, backward, 0)
-        for o in range(1, 4):
-            spot = gw_ref.at[core, lax.rem(i1 + 4 - o, 4)]
-            remote(spot, spot, g1s.at[o - 1], g1r.at[o - 1], axis1[o - 1]).wait()
-        spot = gw_ref.at[core]
-        remote(spot, spot, gcs, gcr, other).start()
+        lax.fori_loop(0, 2, step, 0)
 
     def finish(h, carry):
         for o in offsets:
@@ -402,10 +302,217 @@
             grad_copy(h, o, True).wait_send()
         return carry
 
-    lax.fori_loop(0, heads, finish, 0)
+    def remote(src, dst, s_sem, r_sem, to):
+        return pltpu.make_async_remote_copy(
+            src_ref=src, dst_ref=dst, send_sem=s_sem, recv_sem=r_sem,
+            device_id=to, device_id_type=MESH,
+        )
+
+    def rows_of(i, n):
+        return pl.ds(pl.multiple_of(i * n, n), n)
+
     if REDUCE:
-        spot = gw_ref.at[1 - core]
-        remote(spot, spot, gcs, gcr, other).wait()
+
+        def core_copy(p):
+            return remote(part.at[p, 1 - core], r0.at[p], cs.at[p], cr.at[p], other)
+
+        def first_copies(p):
+            return [
+                remote(
+                    part.at[p, core, rows_of(lax.rem(i1 + o, 4), 64)], r1.at[p, o - 1],
+                    s1s.at[p, o - 1], s1r.at[p, o - 1], axis1[o - 1],
+                )
+                for o in range(1, 4)
+            ]
+
+        def second_copies(p):
+            return [
+                remote(
+                    h1.at[p, rows_of(lax.rem(i2 + o, 4), 16)], r2.at[p, o - 1],
+                    s2s.at[p, o - 1], s2r.at[p, o - 1], axis2[o - 1],
+                )
+                for o in range(1, 4)
+            ]
+
+        def z_copies(p):
+            return [
+                remote(
+                    zsrc.at[p, lax.rem(z + o, 8)], rz.at[p, o - 1],
+                    zs.at[p, o - 1], zr.at[p, o - 1], along_z[o - 1],
+                )
+                for o in range(1, 8)
+            ]
+
+        def z_back(p, to):
+            spots = [zg.at[p, z if to else lax.rem(z + 8 - o, 8)] for o in range(1, 8)]
+            return [
+                remote(spots[o], spots[o], ts.at[p, o], tr.at[p, o], along_z[o])
+                for o in range(7)
+            ]
+
+        def second_back(p, to):
+            spots = [
+                gw_ref.at[p, core, i1, i2 if to else lax.rem(i2 + 4 - o, 4)] for o in range(1, 4)
+            ]
+            return [
+                remote(spots[o], spots[o], g2s.at[p, o], g2r.at[p, o], axis2[o])
+                for o in range(3)
+            ]
+
+        def first_back(p, to):
+            spots = [
+                gw_ref.at[p, core, i1 if to else lax.rem(i1 + 4 - o, 4)] for o in range(1, 4)
+            ]
+            return [
+                remote(spots[o], spots[o], g1s.at[p, o], g1r.at[p, o], axis1[o])
+                for o in range(3)
+            ]
+
+        def core_back(p, to):
+            spot = gw_ref.at[p, core if to else 1 - core]
+            return remote(spot, spot, gcs.at[p], gcr.at[p], other)
+
+        def start_all(copies):
+            for copy in copies:
+                copy.start()
+
+        def wait_all(copies):
+            for copy in copies:
+                copy.wait()
+
+        def to_first(p):
+            core_copy(p).wait()
+
+            def step(i, carry):
+                piece = rows_of(i, 32)
+                total = part[p, core, piece].astype(F32) + r0[p, piece].astype(F32)
+                part[p, core, piece] = total.astype(BF16)
+                return carry
+
+            lax.fori_loop(0, quarter // 32, step, 0)
+            start_all(first_copies(p))
+
+        def to_second(p):
+            wait_all(first_copies(p))
+            for i in range(2):
+                piece = pl.ds(i * 32, 32)
+                mine = pl.ds(pl.multiple_of(i1 * 64 + i * 32, 32), 32)
+                total = part[p, core, mine].astype(F32)
+                for o in range(3):
+                    total = total + r1[p, o, piece].astype(F32)
+                h1[p, piece] = total.astype(BF16)
+            start_all(second_copies(p))
+
+        def to_z(p):
+            wait_all(second_copies(p))
+            total = h1[p, rows_of(i2, 16)].astype(F32)
+            for o in range(3):
+                total = total + r2[p, o].astype(F32)
+            total = total.astype(BF16)
+            for c in range(8):
+                zsrc[p, c] = total[:, c * 256:(c + 1) * 256]
+            start_all(z_copies(p))
+
+        def from_z(p):
+            wait_all(z_copies(p))
+            total = zsrc[p, z].astype(F32)
+            for o in range(7):
+                total = total + rz[p, o].astype(F32)
+            zg[p, z] = total.astype(BF16)
+            start_all(z_back(p, True))
+
+        def from_second(p):
+            wait_all(z_back(p, False))
+            for c in range(8):
+                gw_ref[p, core, i1, i2, :, pl.ds(c * 256, 256)] = zg[p, c]
+            start_all(second_back(p, True))
+
+        def from_first(p):
+            wait_all(second_back(p, False))
+            start_all(first_back(p, True))
+
+        def from_core(p):
+            wait_all(first_back(p, False))
+            core_back(p, True).start()
+
+    def fwd(first, last, more):
+        def step(h, carry):
+            forward(h, lambda: more(h))
+            return carry
+
+        lax.fori_loop(first, last, step, 0)
+
+    def fwd_unpack(first, last, more):
+        def step(h, carry):
+            forward(h, lambda: more(h))
+            unpack_att(h - 2, 0)
+            return carry
+
+        lax.fori_loop(first, last, step, 0)
+
+    def next_qkv(h):
+        start_qkv(h + AHEAD)
+
+    def next_ga(h):
+        start_ga(h + AHEAD - heads)
+
+    def back(first, last):
+        def step(h, carry):
+            backward(h)
+            return carry
+
+        lax.fori_loop(first, last, step, 0)
+
+    def ga_rest(h, carry):
+        start_ga(h)
+        return carry
+
+    fwd(0, 2, next_qkv)
+    fwd_unpack(2, heads - 2, next_qkv)
+    make_part(0)
+    if REDUCE:
+        core_copy(0).start()
+    fwd_unpack(heads - 2, heads - 1, next_ga)
+    if REDUCE:
+        to_first(0)
+    fwd_unpack(heads - 1, heads, next_ga)
+    lax.fori_loop(AHEAD, heads, ga_rest, 0)
+    if REDUCE:
+        to_second(0)
+    back(0, 1)
+    if REDUCE:
+        to_z(0)
+    lax.fori_loop(heads - 2, heads, unpack_att, 0)
+    make_part(1)
+    if not REDUCE:
+        lax.fori_loop(0, lo_ref.shape[1] // wide, make_out, 0)
+        back(1, heads)
+        lax.fori_loop(0, heads, finish, 0)
+    else:
+        core_copy(1).start()
+        back(1, 2)
+        to_first(1)
+        lax.fori_loop(0, lo_ref.shape[1] // wide, make_out, 0)
+        back(2, 3)
+        from_z(0)
+        back(3, 4)
+        to_second(1)
+        to_z(1)
+        from_second(0)
+        back(4, 5)
+        from_first(0)
+        from_z(1)
+        back(5, 6)
+        from_core(0)
+        from_second(1)
+        back(6, 7)
+        from_first(1)
+        back(7, 8)
+        lax.fori_loop(0, heads - 4, finish, 0)
+        from_core(1)
+        lax.fori_loop(heads - 4, heads, finish, 0)
+        core_back(0, False).wait()
+        core_back(1, False).wait()
 
 
 def write_out(*refs):
@@ -455,21 +562,21 @@
     ] + [dma((heads, views))] * 8
     if REDUCE:
         scratch += [
-            pltpu.VMEM((width, model), BF16),
-            pltpu.VMEM((width // 2, model), BF16),
-            pltpu.VMEM((width // 2, model), BF16),
-            pltpu.VMEM((3, 128, model), BF16),
-            pltpu.VMEM((3, 32, model), BF16),
-            pltpu.VMEM((8, 32, model // 8), BF16),
-            pltpu.VMEM((7, 32, model // 8), BF16),
-            pltpu.VMEM((8, 32, model // 8), BF16),
-            dma, dma,
-            dma((3,)), dma((3,)), dma((3,)), dma((3,)),
-            dma((7,)), dma((7,)), dma((7,)), dma((7,)),
-            dma((3,)), dma((3,)), dma((3,)), dma((3,)),
-            dma, dma,
+            pltpu.VMEM((2, 2, width // 4, model), BF16),
+            pltpu.VMEM((2, width // 4, model), BF16),
+            pltpu.VMEM((2, 3, 64, model), BF16),
+            pltpu.VMEM((2, 64, model), BF16),
+            pltpu.VMEM((2, 3, 16, model), BF16),
+            pltpu.VMEM((2, 8, 16, model // 8), BF16),
+            pltpu.VMEM((2, 7, 16, model // 8), BF16),
+            pltpu.VMEM((2, 8, 16, model // 8), BF16),
+            dma((2,)), dma((2,)),
+            dma((2, 3)), dma((2, 3)), dma((2, 3)), dma((2, 3)),
+            dma((2, 7)), dma((2, 7)), dma((2, 7)), dma((2, 7)),
+            dma((2, 3)), dma((2, 3)), dma((2, 3)), dma((2, 3)),
+            dma((2,)), dma((2,)),
         ]
-        gw_shape = jax.ShapeDtypeStruct((2, 4, 4, 32, model), BF16)
+        gw_shape = jax.ShapeDtypeStruct((2, 2, 4, 4, 16, model), BF16)
     else:
         gw_shape = jax.ShapeDtypeStruct((width, model), F32)
     grad_shape = jax.ShapeDtypeStruct(blocks, BF16)

time: 207 us -> 208 us (level)
  Pallas kernels: 204 us -> 207 us
    pallas_call x1, Pallas kernels: 201 us -> 203 us  [body(): pl.pallas_call(functools.partial(kernel, heads, views), out_shape=tuple((...]
where the time goes in v2:
time: 208 us
  Pallas kernels  207 us (100%)
    pallas_call x1, Pallas kernels, body(): pl.pallas_call(functools.partial(kernel, heads, views), out_shape=tuple((...  203 us

profile of v2, /device:TPU:1, one launch (start us, length us, event | category | flops | bytes accessed | tf_op | source)
XLA Modules:
  0.0 207.8 jit_solution(5020108565924800733)
XLA Ops:
  0.6 203.2 %shard_map.110 = (bf16[512,2048]{1,0:T(8,128)(2,1)S(1)}, bf16[4,128,1024]{2,1,0:T(8,128)(2,1)S(1)}, bf16[4,128,1024]{2,1,0:T(8,128)(2,1)S(1)}, bf16[4,128,1024]{...) custom-call(bf16[4,128,1024]{2,1,0:T(8,128)(2,1)} %bitcast.14, bf16[4,128,1024]{2,1,0:T(8,128)(2,1)} %bitcast.15, ...), custom_call_target="tpu_custom_call" | custom-call | flops 9699999744 | bytes 18000000 | tf_op jit(solution)/shard_map/pallas_call | solution.py:587
  203.9 3.8 %shard_map.111 = (bf16[512,2048]{1,0:T(8,128)(2,1)}, bf16[4,128,1024]{2,1,0:T(8,128)(2,1)}, bf16[4,128,1024]{2,1,0:T(8,128)(2,1)}, bf16[4,128,1024]{2,1,0:T(8,128)(2,1)}, bf16[2,2,4,4,16,2048]{5,4,3,2,1,0:T(8,128)(2,1)}) custom-call(bf16[512,2048]{1,0:T(8,128)(2,1)S(1)} %get-tuple-element.15.refs_0_, bf16[4,128,1024]{2,1,0:T(8,128)(2,1)S(1)} %get-tuple-element.16.refs_1_, ...), custom_call_target="tpu_custom_call" | custom-call | tf_op jit(solution)/shard_map/pallas_call | solution.py:606

commit v3 on v1

--- a/solution.py
+++ b/solution.py
@@ -49,7 +49,7 @@
 
     peers = [(scene, at[o]) for o in offsets]
     if REDUCE:
-        part, gsum, r0, r1, r2, zsrc, rz, zg, cs, cr, s1s, s1r, s2s, s2r, zs, zr, ts, tr, g2s, g2r, g1s, g1r, gcs, gcr = reduce_refs
+        part, gsum, r0, r1, r2, zsrc, rz, zp, zx, zg, cs, cr, s1s, s1r, s2s, s2r, zs, zr, xs, xr, ts, tr, g2s, g2r, g1s, g1r, gcs, gcr = reduce_refs
         core = lax.rem(scene, 2)
         x = lax.rem(scene // 2, 4)
         y = lax.rem(scene // 8, 4)
@@ -68,6 +68,20 @@
         for o in range(1, 8):
             zz = lax.rem(z + o, 8)
             along_z.append((place(core, y, x, zz // 4), lax.rem(zz, 4)))
+
+        ring = lax.rem(z + 2, 8)
+        line = ring // 4
+
+        def on_ring(r):
+            zz = lax.rem(r + 6, 8)
+            return place(core, y, x, zz // 4), lax.rem(zz, 4)
+
+        mine_z = (1 - line) * ring + line * (7 - ring)
+        in_line = []
+        for o in range(1, 4):
+            c = lax.rem(mine_z + o, 4)
+            in_line.append(on_ring((1 - line) * c + line * (7 - c)))
+        mirror = on_ring(7 - ring)
         peers = [other] + axis1 + axis2 + along_z
 
     barrier = pltpu.get_barrier_semaphore()
@@ -75,7 +89,7 @@
         pl.semaphore_signal(barrier, inc=1, device_id=peer, device_id_type=MESH)
 
     loads = []
-    for part_id, cols in enumerate((pl.ds(0, 2 * HDIM), pl.ds(2 * HDIM, (heads - 2) * HDIM))):
+    for part_id, cols in enumerate((pl.ds(0, HDIM), pl.ds(HDIM, (heads - 1) * HDIM))):
         for t, ref in enumerate((q_hbm, k_hbm, v_hbm)):
             copy = pltpu.make_async_copy(
                 ref.at[:, :, cols], qkv_in.at[t, :, :, cols], load_sem.at[t, part_id]
@@ -170,10 +184,10 @@
     for copy in loads[:3]:
         copy.wait()
     pl.semaphore_wait(barrier, len(peers))
-    lax.fori_loop(0, 2, send_qkv, 0)
+    lax.fori_loop(0, 1, send_qkv, 0)
     for copy in loads[3:]:
         copy.wait()
-    lax.fori_loop(2, heads, send_qkv, 0)
+    lax.fori_loop(1, heads, send_qkv, 0)
 
     og_load.wait()
     w_load.wait()
@@ -343,45 +357,46 @@
         for o in range(3):
             total = total + r2[o].astype(F32)
         total = total.astype(BF16)
-        for p in range(8):
-            zsrc[p] = total[:, p * 256:(p + 1) * 256]
+        for p in range(4):
+            zsrc[p] = total[:, p * 512:(p + 1) * 512]
         rsz = [
-            remote(zsrc.at[lax.rem(z + o, 8)], rz.at[o - 1], zs.at[o - 1], zr.at[o - 1], along_z[o - 1])
-            for o in range(1, 8)
+            remote(zsrc.at[lax.rem(mine_z + o, 4)], rz.at[o - 1], zs.at[o - 1], zr.at[o - 1], in_line[o - 1])
+            for o in range(1, 4)
         ]
         for copy in rsz:
             copy.start()
         lax.fori_loop(2, 3, backward, 0)
         for copy in rsz:
             copy.wait()
-        total = zsrc[z].astype(F32)
-        for o in range(7):
+        total = zsrc[mine_z].astype(F32)
+        for o in range(3):
             total = total + rz[o].astype(F32)
-        zg[z] = total.astype(BF16)
-        agz = [
-            remote(zg.at[z], zg.at[z], ts.at[o - 1], tr.at[o - 1], along_z[o - 1])
-            for o in range(1, 8)
-        ]
-        for copy in agz:
-            copy.start()
+        zp[...] = total.astype(BF16)
+        across = remote(zp, zx, xs, xr, mirror)
+        across.start()
         lax.fori_loop(3, 4, backward, 0)
-        for o in range(1, 8):
-            src = zg.at[lax.rem(z + 8 - o, 8)]
-            remote(src, src, ts.at[o - 1], tr.at[o - 1], along_z[o - 1]).wait()
-        for p in range(8):
-            gw_ref[core, i1, i2, :, pl.ds(p * 256, 256)] = zg[p]
-        ag2 = []
+        across.wait()
+        zg[mine_z] = (zp[...].astype(F32) + zx[...].astype(F32)).astype(BF16)
+        for o in range(1, 4):
+            spot = zg.at[mine_z]
+            remote(spot, spot, ts.at[o - 1], tr.at[o - 1], in_line[o - 1]).start()
+        lax.fori_loop(4, 5, backward, 0)
+        for o in range(1, 4):
+            spot = zg.at[lax.rem(mine_z + 4 - o, 4)]
+            remote(spot, spot, ts.at[o - 1], tr.at[o - 1], in_line[o - 1]).wait()
+        for p in range(4):
+            gw_ref[core, i1, i2, :, pl.ds(p * 512, 512)] = zg[p]
         for o in range(1, 4):
             spot = gw_ref.at[core, i1, i2]
             remote(spot, spot, g2s.at[o - 1], g2r.at[o - 1], axis2[o - 1]).start()
-        lax.fori_loop(4, 5, backward, 0)
+        lax.fori_loop(5, 6, backward, 0)
         for o in range(1, 4):
             spot = gw_ref.at[core, i1, lax.rem(i2 + 4 - o, 4)]
             remote(spot, spot, g2s.at[o - 1], g2r.at[o - 1], axis2[o - 1]).wait()
         for o in range(1, 4):
             spot = gw_ref.at[core, i1]
             remote(spot, spot, g1s.at[o - 1], g1r.at[o - 1], axis1[o - 1]).start()
-        lax.fori_loop(5, heads, backward, 0)
+        lax.fori_loop(6, heads, backward, 0)
         for o in range(1, 4):
             spot = gw_ref.at[core, lax.rem(i1 + 4 - o, 4)]
             remote(spot, spot, g1s.at[o - 1], g1r.at[o - 1], axis1[o - 1]).wait()
@@ -460,12 +475,14 @@
             pltpu.VMEM((width // 2, model), BF16),
             pltpu.VMEM((3, 128, model), BF16),
             pltpu.VMEM((3, 32, model), BF16),
-            pltpu.VMEM((8, 32, model // 8), BF16),
-            pltpu.VMEM((7, 32, model // 8), BF16),
-            pltpu.VMEM((8, 32, model // 8), BF16),
+            pltpu.VMEM((4, 32, model // 4), BF16),
+            pltpu.VMEM((3, 32, model // 4), BF16),
+            pltpu.VMEM((32, model // 4), BF16),
+            pltpu.VMEM((32, model // 4), BF16),
+            pltpu.VMEM((4, 32, model // 4), BF16),
             dma, dma,
             dma((3,)), dma((3,)), dma((3,)), dma((3,)),
-            dma((7,)), dma((7,)), dma((7,)), dma((7,)),
+            dma((3,)), dma((3,)), dma, dma, dma((3,)), dma((3,)),
             dma((3,)), dma((3,)), dma((3,)), dma((3,)),
             dma, dma,
         ]

time: 207 us -> 204 us (0.986)
  no operation moved by 1% of the time
where the time goes in v3:
time: 204 us; the launch traced here: 203 us
  Pallas kernels  203 us (100%)
    pallas_call x1, Pallas kernels, body(): pl.pallas_call(functools.partial(kernel, heads, views), out_shape=tuple((...  199 us

profile of v3, /device:TPU:1, one launch (start us, length us, event | category | flops | bytes accessed | tf_op | source)
XLA Modules:
  0.0 203.5 jit_solution(1638550133188779620)
XLA Ops:
  0.6 199.1 %shard_map.110 = (bf16[512,2048]{1,0:T(8,128)(2,1)S(1)}, bf16[4,128,1024]{2,1,0:T(8,128)(2,1)S(1)}, bf16[4,128,1024]{2,1,0:T(8,128)(2,1)S(1)}, bf16[4,128,1024]{...) custom-call(bf16[4,128,1024]{2,1,0:T(8,128)(2,1)} %bitcast.14, bf16[4,128,1024]{2,1,0:T(8,128)(2,1)} %bitcast.15, ...), custom_call_target="tpu_custom_call" | custom-call | flops 9699999744 | bytes 18000000 | tf_op jit(solution)/shard_map/pallas_call | solution.py:497
  199.7 3.8 %shard_map.111 = (bf16[512,2048]{1,0:T(8,128)(2,1)}, bf16[4,128,1024]{2,1,0:T(8,128)(2,1)}, bf16[4,128,1024]{2,1,0:T(8,128)(2,1)}, bf16[4,128,1024]{2,1,0:T(8,128)(2,1)}, bf16[2,4,4,32,2048]{4,3,2,1,0:T(8,128)(2,1)}) custom-call(bf16[512,2048]{1,0:T(8,128)(2,1)S(1)} %get-tuple-element.15.refs_0_, bf16[4,128,1024]{2,1,0:T(8,128)(2,1)S(1)} %get-tuple-element.16.refs_1_, ...), custom_call_target="tpu_custom_call" | custom-call | tf_op jit(solution)/shard_map/pallas_call | solution.py:516

commit v4 on v3

--- a/solution.py
+++ b/solution.py
@@ -281,8 +281,11 @@
         lo_ref[:, cols] = dot(att[...], w[:, cols]).astype(BF16)
         return carry
 
+    first_half = 1 - lax.rem(scene, 2)
+
     def make_part(c, carry):
-        span = pl.ds(pl.multiple_of(c * wide, wide), wide)
+        half_at = lax.rem(first_half + c // 2, 2)
+        span = pl.ds(pl.multiple_of((half_at * 2 + lax.rem(c, 2)) * wide, wide), wide)
         for d in range(og.shape[1] // 512):
             cols = pl.ds(d * 512, 512)
             term = dot(att_t[span, :], og[:, cols])
@@ -293,7 +296,7 @@
         return carry
 
     lax.fori_loop(0, heads, unpack_att, 0)
-    lax.fori_loop(0, width // wide, make_part, 0)
+    lax.fori_loop(0, 2, make_part, 0)
     if REDUCE:
         half = width // 2
         core_rows = pl.ds(pl.multiple_of(core * half, half), half)
@@ -307,9 +310,10 @@
 
         c_copy = remote(part.at[other_rows], r0, cs, cr, other)
         c_copy.start()
-    lax.fori_loop(0, lo_ref.shape[1] // wide, make_out, 0)
+    lax.fori_loop(2, 4, make_part, 0)
 
     if not REDUCE:
+        lax.fori_loop(0, lo_ref.shape[1] // wide, make_out, 0)
         lax.fori_loop(0, heads, backward, 0)
     else:
         lax.fori_loop(0, 1, backward, 0)
@@ -333,6 +337,7 @@
         for copy in rs1:
             copy.start()
         lax.fori_loop(1, 2, backward, 0)
+        lax.fori_loop(0, lo_ref.shape[1] // wide, make_out, 0)
         for copy in rs1:
             copy.wait()
 

time: 204 us -> 203 us (level)
    pallas_call x1, Pallas kernels: 199 us -> 197 us  [body(): pl.pallas_call(functools.partial(kernel, heads, views), out_shape=tuple((...]
where the time goes in v4:
time: 203 us; the launch traced here: 201 us
  Pallas kernels  201 us (99%)
    pallas_call x1, Pallas kernels, body(): pl.pallas_call(functools.partial(kernel, heads, views), out_shape=tuple((...  197 us

profile of v4, /device:TPU:1, one launch (start us, length us, event | category | flops | bytes accessed | tf_op | source)
XLA Modules:
  0.0 201.2 jit_solution(1713508854305455642)
XLA Ops:
  0.6 196.8 %shard_map.110 = (bf16[512,2048]{1,0:T(8,128)(2,1)S(1)}, bf16[4,128,1024]{2,1,0:T(8,128)(2,1)S(1)}, bf16[4,128,1024]{2,1,0:T(8,128)(2,1)S(1)}, bf16[4,128,1024]{...) custom-call(bf16[4,128,1024]{2,1,0:T(8,128)(2,1)} %bitcast.14, bf16[4,128,1024]{2,1,0:T(8,128)(2,1)} %bitcast.15, ...), custom_call_target="tpu_custom_call" | custom-call | flops 9699999744 | bytes 18000000 | tf_op jit(solution)/shard_map/pallas_call | solution.py:502
  197.4 3.8 %shard_map.111 = (bf16[512,2048]{1,0:T(8,128)(2,1)}, bf16[4,128,1024]{2,1,0:T(8,128)(2,1)}, bf16[4,128,1024]{2,1,0:T(8,128)(2,1)}, bf16[4,128,1024]{2,1,0:T(8,128)(2,1)}, bf16[2,4,4,32,2048]{4,3,2,1,0:T(8,128)(2,1)}) custom-call(bf16[512,2048]{1,0:T(8,128)(2,1)S(1)} %get-tuple-element.15.refs_0_, bf16[4,128,1024]{2,1,0:T(8,128)(2,1)S(1)} %get-tuple-element.16.refs_1_, ...), custom_call_target="tpu_custom_call" | custom-call | tf_op jit(solution)/shard_map/pallas_call | solution.py:521
